TPU v7x, 32 devices: a whole 2x2x4 slice. The times are simulated.
32 devices in a mesh: groups: 2 (over x), rows: 16 (over z, y, core).
Axes of the slice: x: 2, y: 2, z: 4, core: 2. Of those that a mesh axis runs over, the one named last changes fastest.
Arguments:
- pair: bfloat16 [512, 256, 128], P(('groups', 'rows')), parts along dimension 0, may hold values from -6 to 6
- proj_weights: bfloat16 [6, 128, 128], replicated, may hold values from -0.5 to 0.5
- cotangent: bfloat16 [512, 256, 128], P(('groups', 'rows')), parts along dimension 0, may hold values from -8.5 to 8.5
Outputs:
- update: bfloat16 [512, 256, 128], P(('groups', 'rows')), parts along dimension 0
- pair_grad: bfloat16 [512, 256, 128], P(('groups', 'rows')), parts along dimension 0
- weight_grads: float32 [12, 128, 128], P('groups'), parts along dimension 0
There are 2 independent parts, one for each index of `groups`. A program takes and returns all parts, laid end to end along the dimension named above; an argument that names none is the same for every part. Nothing has to cross between parts.
All inputs are finite; a program needn't handle non-finite values.
Results may differ from a plain program's by a relative error of at most 0.015.
Values may be sent and summed in bfloat16 or wider, within the bound.
A program may use at most 128 MiB of HBM per device.

v0:
```python
import jax
import jax.numpy as jnp
from jax import lax
from jax.sharding import PartitionSpec as P


def layer_norm(values, along_dim):
    centred = values - jnp.mean(values, axis=along_dim, keepdims=True)
    inv_scale = lax.rsqrt(jnp.mean(centred * centred, axis=along_dim, keepdims=True) + 1e-05)
    return (centred * inv_scale, inv_scale)


def norm_backward(normed, inv_scale, upstream, along_dim):
    return (
        upstream
        - jnp.mean(upstream, axis=along_dim, keepdims=True)
        - normed * jnp.mean(upstream * normed, axis=along_dim, keepdims=True)
    ) * inv_scale


def triangle_slab(pieces):
    left_slab, right_slab = pieces
    product = lax.dot_general(
        left_slab, right_slab, (((3,), (3,)), ((0, 1), (0, 1))), preferred_element_type=jnp.float32
    )
    return (product.astype(jnp.bfloat16), left_slab, right_slab)


def edge_backward(upstream, left_slab, right_slab):
    left_part = lax.dot_general(
        upstream, right_slab, (((3,), (2,)), ((0, 1), (0, 1))), preferred_element_type=jnp.float32
    )
    right_part = lax.dot_general(
        upstream, left_slab, (((2,), (2,)), ((0, 1), (0, 1))), preferred_element_type=jnp.float32
    )
    return (left_part.astype(jnp.bfloat16), right_part.astype(jnp.bfloat16))


def body(pair, proj_weights, cotangent):
    residues = pair.shape[1]
    local_rows = pair.shape[0]
    chans = pair.shape[2]
    ranks = lax.axis_size("rows")
    slab_width = chans // ranks
    normed_in, scale_in = layer_norm(pair.astype(jnp.float32), 2)
    normed_bf = normed_in.astype(jnp.bfloat16)
    edge_pre = jnp.einsum(
        "ikd,ndc->ncik", normed_bf, proj_weights[0:4], preferred_element_type=jnp.float32
    )
    gate_pre = jnp.einsum(
        "ikd,dc->ikc", normed_bf, proj_weights[4], preferred_element_type=jnp.float32
    )
    left_sig = jax.nn.sigmoid(edge_pre[1])
    right_sig = jax.nn.sigmoid(edge_pre[3])
    left_edge = (
        (left_sig * edge_pre[0])
        .astype(jnp.bfloat16)
        .reshape(ranks, slab_width, local_rows, residues)
    )
    right_edge = (
        (right_sig * edge_pre[2])
        .astype(jnp.bfloat16)
        .reshape(ranks, slab_width, local_rows, residues)
    )
    products, left_held, right_held = triangle_slab(
        (
            lax.all_to_all(left_edge, "rows", split_axis=0, concat_axis=2, tiled=True),
            lax.all_to_all(right_edge, "rows", split_axis=0, concat_axis=2, tiled=True),
        )
    )
    regrouped = lax.all_to_all(products, "rows", split_axis=2, concat_axis=0, tiled=True).reshape(
        chans, local_rows, residues
    )
    normed_mid, scale_mid = layer_norm(regrouped.astype(jnp.float32), 0)
    mid_bf = normed_mid.astype(jnp.bfloat16)
    projected = jnp.einsum(
        "cij,cd->ijd", mid_bf, proj_weights[5], preferred_element_type=jnp.float32
    )
    gating = jax.nn.sigmoid(gate_pre)
    update = (gating * projected).astype(jnp.bfloat16)
    upstream = cotangent.astype(jnp.float32)
    gated_up = (upstream * gating).astype(jnp.bfloat16)
    gate_grad = (upstream * projected * gating * (1.0 - gating)).astype(jnp.bfloat16)
    out_weights = jnp.stack(
        [
            jnp.einsum("ikd,ikc->dc", normed_bf, gate_grad, preferred_element_type=jnp.float32),
            jnp.einsum("cij,ijd->cd", mid_bf, gated_up, preferred_element_type=jnp.float32),
        ]
    )
    mid_grad = jnp.einsum(
        "ijd,cd->cij", gated_up, proj_weights[5], preferred_element_type=jnp.float32
    )
    prod_grad = norm_backward(normed_mid, scale_mid, mid_grad, 0).astype(jnp.bfloat16)
    prod_grad = prod_grad.reshape(ranks, slab_width, local_rows, residues)
    slab_grad = lax.all_to_all(prod_grad, "rows", split_axis=0, concat_axis=2, tiled=True)
    left_part, right_part = edge_backward(slab_grad, left_held, right_held)
    left_back, right_back = (
        lax.all_to_all(left_part, "rows", split_axis=2, concat_axis=0, tiled=True),
        lax.all_to_all(right_part, "rows", split_axis=2, concat_axis=0, tiled=True),
    )
    left_full = left_back.reshape(chans, local_rows, residues).astype(jnp.float32)
    right_full = right_back.reshape(chans, local_rows, residues).astype(jnp.float32)
    edge_grad = jnp.stack(
        [
            left_full * left_sig,
            left_full * edge_pre[0] * left_sig * (1.0 - left_sig),
            right_full * right_sig,
            right_full * edge_pre[2] * right_sig * (1.0 - right_sig),
        ]
    ).astype(jnp.bfloat16)
    in_weights = jnp.einsum(
        "ikd,ncik->ndc", normed_bf, edge_grad, preferred_element_type=jnp.float32
    )
    input_grad = jnp.einsum(
        "ncik,ndc->ikd", edge_grad, proj_weights[0:4], preferred_element_type=jnp.float32
    )
    input_grad = input_grad + jnp.einsum(
        "ikc,dc->ikd", gate_grad, proj_weights[4], preferred_element_type=jnp.float32
    )
    pair_grad = norm_backward(normed_in, scale_in, input_grad, 2).astype(jnp.bfloat16)
    totals = lax.psum(
        jnp.concatenate([in_weights, out_weights], axis=0).astype(jnp.bfloat16), "rows"
    ).astype(jnp.float32)
    weight_grads = totals / residues
    return (update, pair_grad, weight_grads)


def solution(mesh):
    in_specs = (P(("groups", "rows"), None, None), P(), P(("groups", "rows"), None, None))
    out_specs = (
        P(("groups", "rows"), None, None),
        P(("groups", "rows"), None, None),
        P("groups", None, None),
    )
    return jax.shard_map(body, mesh=mesh, in_specs=in_specs, out_specs=out_specs, check_vma=False)
```

profile of v0, /device:TPU:0, one launch (start us, length us, event | category | flops | bytes accessed | tf_op | source)
XLA Modules:
  0.0 318.2 jit_solution(738744233146156121)
XLA Ops:
  7.2 1.5 copy.69
  8.9 0.3 fusion.9
  9.2 1.3 convolution_bitcast_fusion
  10.5 1.2 fusion.46
  11.7 2.0 copy-done
  13.7 1.1 copy.75
  14.8 7.4 %all-to-all-start.1 = ((bf16[16,8,16,256]{3,1,2,0:T(8,128)(2,1)}), bf16[16,8,16,256]{3,1,2,0:T(8,128)(2,1)S(1)}, u32[]{:S(2)}, u32[]{:S(2)}) async-start(bf16[16,8,16,256]{3,1,2,0:T(8,128)(2,1)} %copy.75), calls=%async_computation.1 | async-start | bytes 2097152 | tf_op jit(solution)/shard_map/all_to_all | solution.py:68
  22.2 1.1 copy.73
  23.3 21.9 %all-to-all-done.1 = bf16[16,8,16,256]{3,1,2,0:T(8,128)(2,1)S(1)} async-done(((bf16[16,8,16,256]{3,1,2,0:T(8,128)(2,1)}), bf16[16,8,16,256]{3,1,2,0:T(8,128)(2,1)S(1)}, u32[]{:S(2)}, u32[]{:S(2)}) %all-to-all-start.1) | async-done | bytes 1048608 | tf_op jit(solution)/shard_map/all_to_all | solution.py:68
  45.2 6.9 %all-to-all-start = ((bf16[16,8,16,256]{3,1,2,0:T(8,128)(2,1)}), bf16[16,8,16,256]{3,1,2,0:T(8,128)(2,1)}, u32[]{:S(2)}, u32[]{:S(2)}) async-start(bf16[16,8,16,256]{3,1,2,0:T(8,128)(2,1)} %copy.73), calls=%async_computation | async-start | bytes 2097152 | tf_op jit(solution)/shard_map/all_to_all | solution.py:67
  52.1 0.2 copy.76
  52.3 22.8 %all-to-all-done = bf16[16,8,16,256]{3,1,2,0:T(8,128)(2,1)} async-done(((bf16[16,8,16,256]{3,1,2,0:T(8,128)(2,1)}), bf16[16,8,16,256]{3,1,2,0:T(8,128)(2,1)}, u32[]{:S(2)}, u32[]{:S(2)}) %all-to-all-start) | async-done | bytes 1048608 | tf_op jit(solution)/shard_map/all_to_all | solution.py:67
  75.1 1.4 copy.74
  76.5 0.5 fusion.34
  77.0 0.6 copy.77
  77.6 31.5 %all_to_all.72 = bf16[1,8,256,256]{3,1,0,2:T(8,128)(2,1)S(1)} all-to-all(bf16[1,8,256,256]{3,1,0,2:T(8,128)(2,1)S(1)} %copy.77), channel_id=1, replica_groups=mesh['groups'=2,'rows'=16] {'rows'}, dimensions={2} | all-to-all | bytes 2097152 | tf_op jit(solution)/shard_map/all_to_all | solution.py:71
  109.1 0.3 convert_bitcast_fusion
  109.6 0.3 multiply_reduce_fusion
  110.0 0.3 multiply_convert_fusion.3
  110.4 0.6 fusion.51
  110.9 0.7 copy-done.7
  111.6 2.5 fusion.13
  114.1 1.6 bitcast_reduce_fusion
  115.8 1.6 fusion.47
  117.5 29.8 %all_to_all.73 = bf16[16,8,16,256]{3,1,2,0:T(8,128)(2,1)S(1)} all-to-all(bf16[16,8,16,256]{3,1,2,0:T(8,128)(2,1)S(1)} %copy.82), channel_id=1, replica_groups=mesh['groups'=2,'rows'=16] {'rows'}, dimensions={0} | all-to-all | bytes 2097152 | tf_op jit(solution)/shard_map/all_to_all | solution.py:95
  147.3 1.0 copy-done.4
  148.6 0.4 fusion.35
  149.0 1.6 copy.84
  150.6 5.0 %all-to-all-start.4 = ((bf16[1,8,256,256]{3,1,0,2:T(8,128)(2,1)}), bf16[1,8,256,256]{3,1,0,2:T(8,128)(2,1)}, u32[]{:S(2)}, u32[]{:S(2)}) async-start(bf16[1,8,256,256]{3,1,0,2:T(8,128)(2,1)} %copy.84), calls=%async_computation.4 | async-start | bytes 2097152 | tf_op jit(solution)/shard_map/all_to_all | solution.py:98
  155.6 2.0 fusion.36
  157.7 1.6 copy.87
  159.3 19.3 %all-to-all-done.4 = bf16[1,8,256,256]{3,1,0,2:T(8,128)(2,1)} async-done(((bf16[1,8,256,256]{3,1,0,2:T(8,128)(2,1)}), bf16[1,8,256,256]{3,1,0,2:T(8,128)(2,1)}, u32[]{:S(2)}, u32[]{:S(2)}) %all-to-all-start.4) | async-done | bytes 1048608 | tf_op jit(solution)/shard_map/all_to_all | solution.py:98
  178.6 6.9 %all-to-all-start.5 = ((bf16[1,8,256,256]{3,1,0,2:T(8,128)(2,1)}), bf16[1,8,256,256]{3,1,0,2:T(8,128)(2,1)}, u32[]{:S(2)}, u32[]{:S(2)}) async-start(bf16[1,8,256,256]{3,1,0,2:T(8,128)(2,1)} %copy.87), calls=%async_computation.5 | async-start | bytes 2097152 | tf_op jit(solution)/shard_map/all_to_all | solution.py:99
  185.5 0.3 all-reduce.2.cloned.1.call-start
  185.8 2.0 fusion.43
  187.8 2.9 fusion.42
  190.7 17.8 %all-to-all-done.5 = bf16[1,8,256,256]{3,1,0,2:T(8,128)(2,1)} async-done(((bf16[1,8,256,256]{3,1,0,2:T(8,128)(2,1)}), bf16[1,8,256,256]{3,1,0,2:T(8,128)(2,1)}, u32[]{:S(2)}, u32[]{:S(2)}) %all-to-all-start.5) | async-done | bytes 1048608 | tf_op jit(solution)/shard_map/all_to_all | solution.py:99
  208.5 5.0 %fusion.24 = (bf16[1,128,16,256]{3,1,0,2:T(8,128)(2,1)S(1)}, bf16[1,128,16,256]{3,1,0,2:T(8,128)(2,1)S(1)}, bf16[1,128,16,256]{3,1,0,2:T(8,128)(2,1)S(1)}, bf16[1,128,16,256]{3,1,0,2:T(8,128)(2,1)S(1)}) fusion(f32[4,128,16,256]{3,1,0,2:T(8,128)} %copy-done, bf16[1,8,16,16,256]{4,1,3,2,0:T(8,128)(2,1)} %bitcast.53, bf16[1,8,16,16,256]{4,1,3,2,0:T(8,128)(2,1)} %bitcast.51), kind=kLoop, calls=%fused_computation.37 | loop fusion | flops 11534336 | bytes 14680064 | tf_op jit(solution)/shard_map/convert.17
  213.5 1.3 fusion.39
  214.8 0.7 fusion.55
  215.5 0.5 copy-done.8
  216.0 0.7 fusion.77
  216.7 0.7 pad_maximum_fusion.3
  217.5 1.6 fusion.8
  219.1 2.3 copy.93
  221.3 88.2 %all-reduce.2.cloned.1.call-done = bf16[6,128,128]{1,2,0:T(8,128)(2,1)} async-done(((bf16[6,128,128]{1,2,0:T(8,128)(2,1)}), bf16[6,128,128]{1,2,0:T(8,128)(2,1)}) %all-reduce.2.cloned.1.call-update) | async-done | bytes 196624 | tf_op jit(solution)/shard_map/psum | solution.py:121
  309.5 1.0 convert_multiply_fusion.2
  310.5 0.9 copy.94
  (29 shorter events, 0.9 us)
Async XLA Ops:
  7.2 2.1 copy-start.9
  10.5 3.2 %copy-start = (f32[4,128,16,256]{3,1,0,2:T(8,128)}, f32[4,128,16,256]{3,1,0,2:T(8,128)S(1)}, u32[]{:S(2)}) copy-start(f32[4,128,16,256]{3,1,0,2:T(8,128)S(1)} %convolution_bitcast_fusion) | copy-start | bytes 25165828
  14.8 30.3 %all-to-all-start.1 = ((bf16[16,8,16,256]{3,1,2,0:T(8,128)(2,1)}), bf16[16,8,16,256]{3,1,2,0:T(8,128)(2,1)S(1)}, u32[]{:S(2)}, u32[]{:S(2)}) async-start(bf16[16,8,16,256]{3,1,2,0:T(8,128)(2,1)} %copy.75), calls=%async_computation.1 | async-start | bytes 2097152 | tf_op jit(solution)/shard_map/all_to_all | solution.py:68
  45.2 29.9 %all-to-all-start = ((bf16[16,8,16,256]{3,1,2,0:T(8,128)(2,1)}), bf16[16,8,16,256]{3,1,2,0:T(8,128)(2,1)}, u32[]{:S(2)}, u32[]{:S(2)}) async-start(bf16[16,8,16,256]{3,1,2,0:T(8,128)(2,1)} %copy.73), calls=%async_computation | async-start | bytes 2097152 | tf_op jit(solution)/shard_map/all_to_all | solution.py:67
  52.3 24.7 %copy-start.2 = (bf16[1,8,16,16,256]{4,3,2,1,0:T(8,128)(2,1)}, bf16[1,8,16,16,256]{4,3,2,1,0:T(8,128)(2,1)S(1)}, u32[]{:S(2)}) copy-start(bf16[1,8,16,16,256]{4,3,2,1,0:T(8,128)(2,1)S(1)} %copy.76) | copy-start | bytes 3145732
  76.5 1.1 copy-start.1
  110.4 1.2 copy-start.7
  114.1 1.6 copy-start.5
  117.5 31.0 %copy-start.3 = (bf16[1,8,16,16,256]{4,3,2,1,0:T(8,128)(2,1)S(1)}, bf16[1,8,16,16,256]{4,3,2,1,0:T(8,128)(2,1)}, u32[]{:S(2)}) copy-start(bf16[1,8,16,16,256]{4,3,2,1,0:T(8,128)(2,1)} %copy-done.2) | copy-start | bytes 3145732
  147.3 1.0 copy-start.4
  150.6 28.0 %all-to-all-start.4 = ((bf16[1,8,256,256]{3,1,0,2:T(8,128)(2,1)}), bf16[1,8,256,256]{3,1,0,2:T(8,128)(2,1)}, u32[]{:S(2)}, u32[]{:S(2)}) async-start(bf16[1,8,256,256]{3,1,0,2:T(8,128)(2,1)} %copy.84), calls=%async_computation.4 | async-start | bytes 2097152 | tf_op jit(solution)/shard_map/all_to_all | solution.py:98
  178.6 29.9 %all-to-all-start.5 = ((bf16[1,8,256,256]{3,1,0,2:T(8,128)(2,1)}), bf16[1,8,256,256]{3,1,0,2:T(8,128)(2,1)}, u32[]{:S(2)}, u32[]{:S(2)}) async-start(bf16[1,8,256,256]{3,1,0,2:T(8,128)(2,1)} %copy.87), calls=%async_computation.5 | async-start | bytes 2097152 | tf_op jit(solution)/shard_map/all_to_all | solution.py:99
  185.5 124.0 %all-reduce.2.cloned.1.call-start = ((), (), s32[]{:S(2)}) async-start(), calls=%async_computation.6 | async-start | bytes 393216 | tf_op jit(solution)/shard_map/psum | solution.py:121
  185.8 2.0 copy-start.6
  214.8 1.2 copy-start.8
Sparse Core Ops, SparseCore 0:
  217.6 91.8 all-reduce.1
where the time goes:
time: 319 us; the launch traced here: 318 us
  waiting for transfers between devices  170 us (53%)
  blocking collectives  61.3 us (19%)
  starting transfers between devices  26.5 us (8%)
  local copies, waits for them, and re-layouts  16.9 us (5%)
  matrix products  16.5 us (5%)
  between operations  14.4 us (5%)
  other arithmetic  12.6 us (4%)
    psum x1, waiting for transfers between devices, body(): lax.psum(jnp.concatenate([in_weights, out_weights], axis=0).astype(jnp.bf...  88.2 us
    all_to_all x1, blocking collectives, body(): lax.all_to_all(products, 'rows', split_axis=2, concat_axis=0, tiled=True)  31.5 us
    all_to_all x1, blocking collectives, body(): lax.all_to_all(prod_grad, 'rows', split_axis=0, concat_axis=2, tiled=True)  29.8 us
    all_to_all x1, waiting for transfers between devices, body(): lax.all_to_all(left_edge, 'rows', split_axis=0, concat_axis=2, tiled=True)  22.8 us
    all_to_all x1, waiting for transfers between devices, body(): lax.all_to_all(right_edge, 'rows', split_axis=0, concat_axis=2, tiled=True)  21.9 us
    all_to_all x1, waiting for transfers between devices, body(): lax.all_to_all(left_part, 'rows', split_axis=2, concat_axis=0, tiled=True)  19.3 us
    all_to_all x1, waiting for transfers between devices, body(): lax.all_to_all(right_part, 'rows', split_axis=2, concat_axis=0, tiled=True)  17.8 us
    unnamed x23, local copies, waits for them, and re-layouts  8.91 us
  transfers between devices with their start and end apart: 5, of which 5 were waited for; matrix products, arithmetic and copies ran while one was open for 4% of the time, Pallas kernels for 0%

commit v1 on v0

--- a/solution.py
+++ b/solution.py
@@ -1,7 +1,14 @@
+import functools
+
 import jax
 import jax.numpy as jnp
 from jax import lax
+from jax.experimental import pallas as pl
+from jax.experimental.pallas import tpu as pltpu
 from jax.sharding import PartitionSpec as P
+
+VMEM_LIMIT = 48 * 1024 * 1024
+CHUNKS = 4
 
 
 def layer_norm(values, along_dim):
@@ -18,22 +25,256 @@
     ) * inv_scale
 
 
-def triangle_slab(pieces):
-    left_slab, right_slab = pieces
-    product = lax.dot_general(
-        left_slab, right_slab, (((3,), (3,)), ((0, 1), (0, 1))), preferred_element_type=jnp.float32
-    )
-    return (product.astype(jnp.bfloat16), left_slab, right_slab)
-
-
-def edge_backward(upstream, left_slab, right_slab):
-    left_part = lax.dot_general(
-        upstream, right_slab, (((3,), (2,)), ((0, 1), (0, 1))), preferred_element_type=jnp.float32
-    )
-    right_part = lax.dot_general(
-        upstream, left_slab, (((2,), (2,)), ((0, 1), (0, 1))), preferred_element_type=jnp.float32
-    )
-    return (left_part.astype(jnp.bfloat16), right_part.astype(jnp.bfloat16))
+def meet(n, me):
+    barrier = pltpu.get_barrier_semaphore()
+
+    @pl.loop(1, n)
+    def _(s):
+        pl.semaphore_signal(
+            barrier,
+            inc=1,
+            device_id={"rows": lax.rem(me + s, n)},
+            device_id_type=pl.DeviceIdType.MESH,
+        )
+
+    pl.semaphore_wait(barrier, n - 1)
+
+
+def send(src, dst, send_sem, recv_sem, rank):
+    pltpu.make_async_remote_copy(
+        src_ref=src,
+        dst_ref=dst,
+        send_sem=send_sem,
+        recv_sem=recv_sem,
+        device_id={"rows": rank},
+        device_id_type=pl.DeviceIdType.MESH,
+    ).start()
+
+
+def drain(ref, sem):
+    pltpu.make_async_copy(ref, ref, sem).wait()
+
+
+def forward_kernel(
+    n, left, right, regrouped, left_held, right_held, products, send_sem, recv_sem, back_send, back_recv
+):
+    me = lax.axis_index("rows")
+    width, rows = left.shape[1], left.shape[2]
+    chunks = recv_sem.shape[1]
+    per = width // chunks
+    meet(n, me)
+    mine = pl.ds(me * rows, rows)
+    for g in range(chunks):
+        part = pl.ds(g * per, per)
+        for a, (src, dst) in enumerate(((left, left_held), (right, right_held))):
+            pltpu.make_async_copy(
+                src.at[me, part], dst.at[part, mine, :], recv_sem.at[a, g]
+            ).start()
+
+        @pl.loop(1, n)
+        def _(s):
+            rank = lax.rem(me + s, n)
+            for a, (src, dst) in enumerate(((left, left_held), (right, right_held))):
+                send(
+                    src.at[rank, part],
+                    dst.at[part, mine, :],
+                    send_sem.at[a],
+                    recv_sem.at[a, g],
+                    rank,
+                )
+
+    for g in range(chunks):
+        part = pl.ds(g * per, per)
+        drain(left_held.at[part], recv_sem.at[0, g])
+        drain(right_held.at[part], recv_sem.at[1, g])
+
+        @pl.loop(g * per, (g + 1) * per)
+        def _(c):
+            products[c] = lax.dot_general(
+                left_held[c], right_held[c], (((1,), (1,)), ((), ())),
+                preferred_element_type=jnp.float32,
+            ).astype(jnp.bfloat16)
+
+        pltpu.make_async_copy(
+            products.at[part, mine, :], regrouped.at[me, part], back_recv
+        ).start()
+
+        @pl.loop(1, n)
+        def _(s):
+            rank = lax.rem(me + s, n)
+            send(
+                products.at[part, pl.ds(rank * rows, rows), :],
+                regrouped.at[me, part],
+                back_send,
+                back_recv,
+                rank,
+            )
+
+    drain(regrouped, back_recv)
+    others = pl.ds(0, n - 1)
+    drain(left.at[others], send_sem.at[0])
+    drain(right.at[others], send_sem.at[1])
+    drain(left.at[others], back_send)
+
+
+def backward_kernel(
+    n, grad, left_held, right_held, left_back, right_back,
+    held, left_part, right_part, send_sem, recv_sem, back_send, back_recv
+):
+    me = lax.axis_index("rows")
+    width, rows = grad.shape[1], grad.shape[2]
+    chunks = recv_sem.shape[0]
+    per = width // chunks
+    meet(n, me)
+    mine = pl.ds(me * rows, rows)
+    for g in range(chunks):
+        part = pl.ds(g * per, per)
+        pltpu.make_async_copy(grad.at[me, part], held.at[part, mine, :], recv_sem.at[g]).start()
+
+        @pl.loop(1, n)
+        def _(s):
+            rank = lax.rem(me + s, n)
+            send(grad.at[rank, part], held.at[part, mine, :], send_sem, recv_sem.at[g], rank)
+
+    for g in range(chunks):
+        part = pl.ds(g * per, per)
+        drain(held.at[part], recv_sem.at[g])
+
+        @pl.loop(g * per, (g + 1) * per)
+        def _(c):
+            left_part[c] = lax.dot_general(
+                held[c], right_held[c], (((1,), (0,)), ((), ())),
+                preferred_element_type=jnp.float32,
+            ).astype(jnp.bfloat16)
+            right_part[c] = lax.dot_general(
+                held[c], left_held[c], (((0,), (0,)), ((), ())),
+                preferred_element_type=jnp.float32,
+            ).astype(jnp.bfloat16)
+
+        both = ((left_part, left_back), (right_part, right_back))
+        for a, (src, dst) in enumerate(both):
+            pltpu.make_async_copy(
+                src.at[part, mine, :], dst.at[me, part], back_recv.at[a]
+            ).start()
+
+        @pl.loop(1, n)
+        def _(s):
+            rank = lax.rem(me + s, n)
+            for a, (src, dst) in enumerate(both):
+                send(
+                    src.at[part, pl.ds(rank * rows, rows), :],
+                    dst.at[me, part],
+                    back_send.at[a],
+                    back_recv.at[a],
+                    rank,
+                )
+
+    drain(left_back, back_recv.at[0])
+    drain(right_back, back_recv.at[1])
+    others = pl.ds(0, n - 1)
+    drain(grad.at[others], send_sem)
+    drain(grad.at[others], back_send.at[0])
+    drain(grad.at[others], back_send.at[1])
+
+
+def totals_kernel(n, shares, totals, landed, mine, send_sem, recv_sem, back_send, back_recv):
+    me = lax.axis_index("rows")
+    meet(n, me)
+    pltpu.make_async_copy(shares.at[me], landed.at[me], recv_sem).start()
+
+    @pl.loop(1, n)
+    def _(s):
+        rank = lax.rem(me + s, n)
+        send(shares.at[rank], landed.at[me], send_sem, recv_sem, rank)
+
+    drain(landed, recv_sem)
+    mine[...] = jnp.sum(landed[...].astype(jnp.float32), axis=0).astype(mine.dtype)
+    pltpu.make_async_copy(mine, totals.at[me], back_recv).start()
+
+    @pl.loop(1, n)
+    def _(s):
+        rank = lax.rem(me + s, n)
+        send(mine, totals.at[me], back_send, back_recv, rank)
+
+    drain(totals, back_recv)
+    others = pl.ds(0, n - 1)
+    drain(shares.at[others], send_sem)
+    drain(shares.at[others], back_send)
+
+
+def in_vmem(count):
+    return [pl.BlockSpec(memory_space=pltpu.VMEM)] * count
+
+
+def params(collective_id):
+    return pltpu.CompilerParams(
+        collective_id=collective_id, has_side_effects=True, vmem_limit_bytes=VMEM_LIMIT
+    )
+
+
+def exchange_forward(left, right):
+    n, width, rows, residues = left.shape
+    chunks = min(CHUNKS, width)
+    slab = jax.ShapeDtypeStruct((width, n * rows, residues), jnp.bfloat16)
+    whole = jax.ShapeDtypeStruct((width, n * rows, n * rows), jnp.bfloat16)
+    return pl.pallas_call(
+        functools.partial(forward_kernel, n),
+        out_shape=[jax.ShapeDtypeStruct((n, width, rows, n * rows), jnp.bfloat16), slab, slab],
+        in_specs=in_vmem(2),
+        out_specs=in_vmem(3),
+        scratch_shapes=[
+            pltpu.VMEM(whole.shape, jnp.bfloat16),
+            pltpu.SemaphoreType.DMA((2,)),
+            pltpu.SemaphoreType.DMA((2, chunks)),
+            pltpu.SemaphoreType.DMA,
+            pltpu.SemaphoreType.DMA,
+        ],
+        compiler_params=params(0),
+    )(left, right)
+
+
+def exchange_backward(grad, left_held, right_held):
+    n, width, rows, residues = grad.shape
+    chunks = min(CHUNKS, width)
+    slab = (width, n * rows, residues)
+    back = jax.ShapeDtypeStruct((n, width, rows, residues), jnp.bfloat16)
+    return pl.pallas_call(
+        functools.partial(backward_kernel, n),
+        out_shape=[back, back],
+        in_specs=in_vmem(3),
+        out_specs=in_vmem(2),
+        scratch_shapes=[pltpu.VMEM(slab, jnp.bfloat16)] * 3
+        + [
+            pltpu.SemaphoreType.DMA,
+            pltpu.SemaphoreType.DMA((chunks,)),
+            pltpu.SemaphoreType.DMA((2,)),
+            pltpu.SemaphoreType.DMA((2,)),
+        ],
+        compiler_params=params(1),
+    )(grad, left_held, right_held)
+
+
+def sum_over_rows(shares, n):
+    count, chans, _ = shares.shape
+    rows = count * chans // n
+    dtype = jnp.bfloat16 if rows % 16 == 0 else jnp.float32
+    shares = shares.astype(jnp.bfloat16).astype(dtype).reshape(n, rows, chans)
+    totals = pl.pallas_call(
+        functools.partial(totals_kernel, n),
+        out_shape=jax.ShapeDtypeStruct(shares.shape, dtype),
+        in_specs=in_vmem(1),
+        out_specs=pl.BlockSpec(memory_space=pltpu.VMEM),
+        scratch_shapes=[
+            pltpu.VMEM(shares.shape, dtype),
+            pltpu.VMEM((rows, chans), dtype),
+            pltpu.SemaphoreType.DMA,
+            pltpu.SemaphoreType.DMA,
+            pltpu.SemaphoreType.DMA,
+            pltpu.SemaphoreType.DMA,
+        ],
+        compiler_params=params(2),
+    )(shares)
+    return totals.reshape(count, chans, chans).astype(jnp.float32)
 
 
 def body(pair, proj_weights, cotangent):
@@ -62,15 +303,8 @@
         .astype(jnp.bfloat16)
         .reshape(ranks, slab_width, local_rows, residues)
     )
-    products, left_held, right_held = triangle_slab(
-        (
-            lax.all_to_all(left_edge, "rows", split_axis=0, concat_axis=2, tiled=True),
-            lax.all_to_all(right_edge, "rows", split_axis=0, concat_axis=2, tiled=True),
-        )
-    )
-    regrouped = lax.all_to_all(products, "rows", split_axis=2, concat_axis=0, tiled=True).reshape(
-        chans, local_rows, residues
-    )
+    regrouped, left_held, right_held = exchange_forward(left_edge, right_edge)
+    regrouped = regrouped.reshape(chans, local_rows, residues)
     normed_mid, scale_mid = layer_norm(regrouped.astype(jnp.float32), 0)
     mid_bf = normed_mid.astype(jnp.bfloat16)
     projected = jnp.einsum(
@@ -92,12 +326,7 @@
     )
     prod_grad = norm_backward(normed_mid, scale_mid, mid_grad, 0).astype(jnp.bfloat16)
     prod_grad = prod_grad.reshape(ranks, slab_width, local_rows, residues)
-    slab_grad = lax.all_to_all(prod_grad, "rows", split_axis=0, concat_axis=2, tiled=True)
-    left_part, right_part = edge_backward(slab_grad, left_held, right_held)
-    left_back, right_back = (
-        lax.all_to_all(left_part, "rows", split_axis=2, concat_axis=0, tiled=True),
-        lax.all_to_all(right_part, "rows", split_axis=2, concat_axis=0, tiled=True),
-    )
+    left_back, right_back = exchange_backward(prod_grad, left_held, right_held)
     left_full = left_back.reshape(chans, local_rows, residues).astype(jnp.float32)
     right_full = right_back.reshape(chans, local_rows, residues).astype(jnp.float32)
     edge_grad = jnp.stack(
@@ -118,9 +347,7 @@
         "ikc,dc->ikd", gate_grad, proj_weights[4], preferred_element_type=jnp.float32
     )
     pair_grad = norm_backward(normed_in, scale_in, input_grad, 2).astype(jnp.bfloat16)
-    totals = lax.psum(
-        jnp.concatenate([in_weights, out_weights], axis=0).astype(jnp.bfloat16), "rows"
-    ).astype(jnp.float32)
+    totals = sum_over_rows(jnp.concatenate([in_weights, out_weights], axis=0), ranks)
     weight_grads = totals / residues
     return (update, pair_grad, weight_grads)
 

time: 319 us -> 190 us (0.60)
  waiting for transfers between devices: 170 us -> 0 us
  Pallas kernels: 0 us -> 162 us
  blocking collectives: 61.3 us -> 0 us
  starting transfers between devices: 26.5 us -> 0 us
  between operations: 14.4 us -> 0.87 us
  local copies, waits for them, and re-layouts: 16.9 us -> 5.27 us
  matrix products: 16.5 us -> 10.6 us
    pallas_call x0 -> x3, Pallas kernels: none -> 162 us  [the longest x1 73.2 us: exchange_forward(): pl.pallas_call(functools.partial(forward_kernel, n), out_shape=[jax.Shape...]
    psum x1 -> x0, waiting for transfers between devices: 88.2 us -> none  [body(): lax.psum(jnp.concatenate([in_weights, out_weights], axis=0).astype(jnp.bf...]
    all_to_all x4 -> x0, waiting for transfers between devices: 81.8 us -> none  [the longest x1 22.8 us: body(): lax.all_to_all(left_edge, 'rows', split_axis=0, concat_axis=2, tiled=True)]
    all_to_all x2 -> x0, blocking collectives: 61.3 us -> none  [the longest x1 31.5 us: body(): lax.all_to_all(products, 'rows', split_axis=2, concat_axis=0, tiled=True)]
    all_to_all x4 -> x0, starting transfers between devices: 26.3 us -> none  [the longest x1 7.39 us: body(): lax.all_to_all(right_edge, 'rows', split_axis=0, concat_axis=2, tiled=True)]
    unnamed x23 -> x6, local copies, waits for them, and re-layouts: 8.91 us -> 3.51 us
    convert_element_type x4 -> x1, local copies, waits for them, and re-layouts: 3.86 us -> 0.59 us  [body(): norm_backward(normed_mid, scale_mid, mid_grad, 0).astype(jnp.bfloat16)]
  transfers between devices with their start and end apart: 5 -> 0, of which waited for: 5 -> 0; matrix products, arithmetic and copies ran while one was open for 4% -> 0% of each run, Pallas kernels for 0% -> 0%
where the time goes in v1:
time: 190 us
  Pallas kernels  162 us (85%)
  other arithmetic  12 us (6%)
  matrix products  10.6 us (6%)
  local copies, waits for them, and re-layouts  5.27 us (3%)
    pallas_call x1, Pallas kernels, exchange_forward(): pl.pallas_call(functools.partial(forward_kernel, n), out_shape=[jax.Shape...  73.2 us
    pallas_call x1, Pallas kernels, exchange_backward(): pl.pallas_call(functools.partial(backward_kernel, n), out_shape=[back, ba...  69.9 us
    pallas_call x1, Pallas kernels, sum_over_rows(): pl.pallas_call(functools.partial(totals_kernel, n), out_shape=jax.ShapeDt...  18.5 us
    another operation x1, other arithmetic  5.57 us

profile of v1, /device:TPU:0, one launch (start us, length us, event | category | flops | bytes accessed | tf_op | source)
XLA Modules:
  0.0 190.2 jit_solution(10828929725142641796)
XLA Ops:
  0.6 0.0 copy-start.1
  0.6 1.5 copy.6
  2.2 0.2 convert_reduce_fusion
  2.4 0.3 fusion.9
  2.7 0.0 copy-done.1
  2.7 1.3 convolution_bitcast_fusion
  4.0 1.1 multiply_convert_fusion
  5.1 0.6 copy.11
  5.7 0.6 copy.10
  6.3 73.2 %shard_map.58 = (bf16[16,8,16,256]{3,2,1,0:T(8,128)(2,1)S(1)}, bf16[8,256,256]{2,1,0:T(8,128)(2,1)S(1)}, bf16[8,256,256]{2,1,0:T(8,128)(2,1)S(1)}) custom-call(bf16[16,8,16,256]{3,2,1,0:T(8,128)(2,1)S(1)} %bitcast.98, bf16[16,8,16,256]{3,2,1,0:T(8,128)(2,1)S(1)} %bitcast.97), custom_call_target="tpu_custom_call" | custom-call | tf_op jit(solution)/shard_map/pallas_call | solution.py:220
  79.5 0.2 convert_reduce_fusion.1
  79.7 0.3 multiply_reduce_fusion
  80.0 0.3 multiply_convert_fusion.7
  80.3 0.3 bitcast_convert_fusion.2
  80.6 0.0 copy-start
  80.7 0.6 fusion.35
  81.2 0.7 copy-done
  81.9 2.2 %fusion.13 = (bf16[16,256,128]{2,1,0:T(8,128)(2,1)S(1)}, bf16[16,256,128]{2,1,0:T(8,128)(2,1)}, f32[16,256,128]{2,1,0:T(8,128)S(1)}) fusion(f32[16,256,128]{2,1,0:T(8,128)S(1)} %fusion.35, bf16[16,256,128]{2,1,0:T(8,128)(2,1)S(1)} %copy-done, bf16[6,128,128]{2,1,0:T(8,128)(2,1)S(1)} %copy-done.1, bf16[16,256,128]{1,2,0:T(8,128)(2,1)S(1)} %copy.6, ...), kind=kOutput, calls=%fused_computation.19 | convolution fusion | flops 142082048 | bytes 8454144 | tf_op jit(solution)/shard_map/ikd,dc->ikc/dot_general | solution.py:291
  84.1 0.4 fusion.31
  84.5 1.5 fusion.30
  86.0 1.7 bitcast_reduce_fusion
  87.7 1.7 fusion.22
  89.4 0.6 copy.14
  90.0 69.9 %shard_map.59 = (bf16[16,8,16,256]{3,2,1,0:T(8,128)(2,1)S(1)}, bf16[16,8,16,256]{3,2,1,0:T(8,128)(2,1)S(1)}) custom-call(bf16[16,8,16,256]{3,2,1,0:T(8,128)(2,1)S(1)} %bitcast.96, bf16[8,256,256]{2,1,0:T(8,128)(2,1)S(1)} %get-tuple-element.9.left_held, bf16[8,256,256]{2,1,0:T(8,128)(2,1)S(1)} %get-tuple-element.10.right_held), custom_call_target="tpu_custom_call" | custom-call | tf_op jit(solution)/shard_map/pallas_call | solution.py:241
  159.9 0.3 bitcast_convert_fusion
  160.2 0.3 bitcast_convert_fusion.1
  160.5 5.6 %multiply_convert_fusion.5 = (bf16[1,128,16,256]{3,1,0,2:T(8,128)(2,1)S(1)}, bf16[1,128,16,256]{3,1,0,2:T(8,128)(2,1)S(1)}, bf16[1,128,16,256]{3,1,0,2:T(8,128)(2,1)S(1)}, bf16[1,128,16,256]{3,1,0,2:T(8,128)(2,1)S(1)}) fusion(f32[1,128,16,256]{3,2,1,0:T(8,128)S(1)} %bitcast_convert_fusion.1, f32[4,128,16,256]{3,1,0,2:T(8,128)S(1)} %convolution_bitcast_fusion, ...), kind=kLoop, calls=%fused_computation.43 | loop fusion | flops 10485760 | bytes 16777216 | tf_op jit(solution)/shard_map/convert.9
  166.1 1.5 fusion.27
  167.6 0.7 fusion.39
  168.3 0.7 fusion.61
  169.0 18.5 %shard_map.60 = bf16[16,48,128]{2,1,0:T(8,128)(2,1)S(1)} custom-call(bf16[16,48,128]{2,1,0:T(8,128)(2,1)S(1)} %bitcast.101), custom_call_target="tpu_custom_call" | custom-call | tf_op jit(solution)/shard_map/pallas_call | solution.py:262
  187.5 0.6 fusion.8
  188.1 1.3 copy.21
  189.4 0.8 convert_multiply_fusion.2
  (8 shorter events, 0.1 us)
Async XLA Ops:
  0.6 2.1 %copy-start.1 = (bf16[6,128,128]{2,1,0:T(8,128)(2,1)S(1)}, bf16[6,128,128]{2,1,0:T(8,128)(2,1)}, u32[]{:S(2)}) copy-start(bf16[6,128,128]{2,1,0:T(8,128)(2,1)} %param.4) | copy-start | bytes 589828
  80.6 1.2 copy-start

commit v2 on v1

--- a/solution.py
+++ b/solution.py
@@ -8,7 +8,7 @@
 from jax.sharding import PartitionSpec as P
 
 VMEM_LIMIT = 48 * 1024 * 1024
-CHUNKS = 4
+CHUNKS = 8
 
 
 def layer_norm(values, along_dim):
@@ -55,126 +55,193 @@
     pltpu.make_async_copy(ref, ref, sem).wait()
 
 
+def place(n):
+    me = lax.axis_index("rows")
+    half = lax.div(me, n // 2)
+    first = half * (n // 2)
+    hub = n // 4 * (1 + half)
+    is_hub = jnp.logical_and(me >= hub, me < hub + n // 4)
+    partner = me + n // 4 * (1 - 2 * half)
+    return me, half, first, hub, is_hub, partner
+
+
+def to_hubs(me, hub, hubs, is_hub, pairs, part, send_sems, recv_sems):
+    @pl.loop(0, hubs)
+    def _(s):
+        q = lax.rem(me + s, hubs)
+
+        @pl.when(hub + q != me)
+        def _():
+            for (src, dst), sent, came in zip(pairs, send_sems, recv_sems):
+                send(src.at[q, part], dst, sent, came, hub + q)
+
+    @pl.when(is_hub)
+    def _():
+        for (src, dst), came in zip(pairs, recv_sems):
+            pltpu.make_async_copy(src.at[me - hub, part], dst, came).start()
+
+
+def from_hub(me, first, hub, members, rows, pairs, part, send_sems, recv_sems):
+    for (src, dst), came in zip(pairs, recv_sems):
+        pltpu.make_async_copy(
+            src.at[part, pl.ds((me - first) * rows, rows), :], dst.at[me - hub, part], came
+        ).start()
+
+    @pl.loop(1, members)
+    def _(s):
+        member = lax.rem(me - first + s, members)
+        for (src, dst), sent, came in zip(pairs, send_sems, recv_sems):
+            send(
+                src.at[part, pl.ds(member * rows, rows), :],
+                dst.at[me - hub, part],
+                sent,
+                came,
+                first + member,
+            )
+
+
 def forward_kernel(
-    n, left, right, regrouped, left_held, right_held, products, send_sem, recv_sem, back_send, back_recv
+    n, left, right, regrouped, left_held, right_held, products,
+    send_sem, recv_sem, swap_send, swap_recv, back_send, back_recv
 ):
-    me = lax.axis_index("rows")
-    width, rows = left.shape[1], left.shape[2]
-    chunks = recv_sem.shape[1]
+    me, half, first, hub, is_hub, partner = place(n)
+    hubs, width, rows, _ = left.shape
+    members = n // 2
+    chunks = swap_recv.shape[0]
     per = width // chunks
     meet(n, me)
-    mine = pl.ds(me * rows, rows)
+    own_rows = pl.ds(first * rows, members * rows)
+    far_rows = pl.ds((members - first) * rows, members * rows)
     for g in range(chunks):
         part = pl.ds(g * per, per)
-        for a, (src, dst) in enumerate(((left, left_held), (right, right_held))):
-            pltpu.make_async_copy(
-                src.at[me, part], dst.at[part, mine, :], recv_sem.at[a, g]
-            ).start()
-
-        @pl.loop(1, n)
-        def _(s):
-            rank = lax.rem(me + s, n)
-            for a, (src, dst) in enumerate(((left, left_held), (right, right_held))):
-                send(
-                    src.at[rank, part],
-                    dst.at[part, mine, :],
-                    send_sem.at[a],
-                    recv_sem.at[a, g],
-                    rank,
+        pairs = (
+            (right, right_held.at[part, pl.ds(me * rows, rows), :]),
+            (left, left_held.at[part, pl.ds((me - first) * rows, rows), :]),
+        )
+        to_hubs(
+            me, hub, hubs, is_hub, pairs, part,
+            (send_sem.at[1], send_sem.at[0]), (recv_sem.at[1, g], recv_sem.at[0, g]),
+        )
+
+    @pl.when(is_hub)
+    def _():
+        for g in range(chunks + 1):
+            if g < chunks:
+                part = pl.ds(g * per, per)
+                block = right_held.at[part, own_rows, :]
+                drain(block, recv_sem.at[1, g])
+                send(block, block, swap_send, swap_recv.at[g], partner)
+            if g > 0:
+                done = pl.ds((g - 1) * per, per)
+                drain(left_held.at[done], recv_sem.at[0, g - 1])
+                drain(right_held.at[done, far_rows, :], swap_recv.at[g - 1])
+
+                @pl.loop((g - 1) * per, g * per)
+                def _(c):
+                    products[c] = lax.dot_general(
+                        left_held[c], right_held[c], (((1,), (1,)), ((), ())),
+                        preferred_element_type=jnp.float32,
+                    ).astype(jnp.bfloat16)
+
+                from_hub(
+                    me, first, hub, members, rows, ((products, regrouped),), done,
+                    (back_send,), (back_recv,),
                 )
 
+    drain(regrouped, back_recv)
+
+    @pl.when(is_hub)
+    def _():
+        others = pl.ds(0, hubs - 1)
+        drain(left.at[others], send_sem.at[0])
+        drain(right.at[others], send_sem.at[1])
+        drain(left_held, swap_send)
+        drain(products.at[:, pl.ds(0, (members - 1) * rows), :], back_send)
+
+    @pl.when(jnp.logical_not(is_hub))
+    def _():
+        drain(left, send_sem.at[0])
+        drain(right, send_sem.at[1])
+
+
+def backward_kernel(
+    n, grad, left_held, right_held, left_back, right_back,
+    held, left_part, kept, away, landed,
+    send_sem, recv_sem, swap_send, swap_recv, back_send, back_recv
+):
+    me, half, first, hub, is_hub, partner = place(n)
+    hubs, width, rows, _ = grad.shape
+    members = n // 2
+    chunks = swap_recv.shape[0]
+    per = width // chunks
+    meet(n, me)
+    span = members * rows
+    own_cols = pl.ds(pl.multiple_of(first * rows, span), span)
+    far_cols = pl.ds(pl.multiple_of((members - first) * rows, span), span)
     for g in range(chunks):
         part = pl.ds(g * per, per)
-        drain(left_held.at[part], recv_sem.at[0, g])
-        drain(right_held.at[part], recv_sem.at[1, g])
-
-        @pl.loop(g * per, (g + 1) * per)
-        def _(c):
-            products[c] = lax.dot_general(
-                left_held[c], right_held[c], (((1,), (1,)), ((), ())),
-                preferred_element_type=jnp.float32,
-            ).astype(jnp.bfloat16)
-
-        pltpu.make_async_copy(
-            products.at[part, mine, :], regrouped.at[me, part], back_recv
-        ).start()
-
-        @pl.loop(1, n)
-        def _(s):
-            rank = lax.rem(me + s, n)
-            send(
-                products.at[part, pl.ds(rank * rows, rows), :],
-                regrouped.at[me, part],
-                back_send,
-                back_recv,
-                rank,
-            )
-
-    drain(regrouped, back_recv)
-    others = pl.ds(0, n - 1)
-    drain(left.at[others], send_sem.at[0])
-    drain(right.at[others], send_sem.at[1])
-    drain(left.at[others], back_send)
-
-
-def backward_kernel(
-    n, grad, left_held, right_held, left_back, right_back,
-    held, left_part, right_part, send_sem, recv_sem, back_send, back_recv
-):
-    me = lax.axis_index("rows")
-    width, rows = grad.shape[1], grad.shape[2]
-    chunks = recv_sem.shape[0]
-    per = width // chunks
-    meet(n, me)
-    mine = pl.ds(me * rows, rows)
-    for g in range(chunks):
-        part = pl.ds(g * per, per)
-        pltpu.make_async_copy(grad.at[me, part], held.at[part, mine, :], recv_sem.at[g]).start()
-
-        @pl.loop(1, n)
-        def _(s):
-            rank = lax.rem(me + s, n)
-            send(grad.at[rank, part], held.at[part, mine, :], send_sem, recv_sem.at[g], rank)
-
-    for g in range(chunks):
-        part = pl.ds(g * per, per)
-        drain(held.at[part], recv_sem.at[g])
-
-        @pl.loop(g * per, (g + 1) * per)
-        def _(c):
-            left_part[c] = lax.dot_general(
-                held[c], right_held[c], (((1,), (0,)), ((), ())),
-                preferred_element_type=jnp.float32,
-            ).astype(jnp.bfloat16)
-            right_part[c] = lax.dot_general(
-                held[c], left_held[c], (((0,), (0,)), ((), ())),
-                preferred_element_type=jnp.float32,
-            ).astype(jnp.bfloat16)
-
-        both = ((left_part, left_back), (right_part, right_back))
-        for a, (src, dst) in enumerate(both):
-            pltpu.make_async_copy(
-                src.at[part, mine, :], dst.at[me, part], back_recv.at[a]
-            ).start()
-
-        @pl.loop(1, n)
-        def _(s):
-            rank = lax.rem(me + s, n)
-            for a, (src, dst) in enumerate(both):
-                send(
-                    src.at[part, pl.ds(rank * rows, rows), :],
-                    dst.at[me, part],
-                    back_send.at[a],
-                    back_recv.at[a],
-                    rank,
+        pairs = ((grad, held.at[part, pl.ds((me - first) * rows, rows), :]),)
+        to_hubs(me, hub, hubs, is_hub, pairs, part, (send_sem,), (recv_sem.at[g],))
+
+    def outer(upstream, values):
+        return lax.dot_general(
+            upstream, values, (((0,), (0,)), ((), ())), preferred_element_type=jnp.float32
+        ).astype(jnp.bfloat16)
+
+    @pl.when(is_hub)
+    def _():
+        for g in range(chunks + 1):
+            if g < chunks:
+                part = pl.ds(g * per, per)
+                drain(held.at[part], recv_sem.at[g])
+
+                @pl.loop(g * per, (g + 1) * per)
+                def _(c):
+                    away[c] = outer(held[c, :, far_cols], left_held[c])
+
+                send(away.at[part], landed.at[part], swap_send, swap_recv.at[g], partner)
+
+                @pl.loop(g * per, (g + 1) * per)
+                def _(c):
+                    left_part[c] = lax.dot_general(
+                        held[c], right_held[c], (((1,), (0,)), ((), ())),
+                        preferred_element_type=jnp.float32,
+                    ).astype(jnp.bfloat16)
+                    kept[c] = outer(held[c, :, own_cols], left_held[c])
+
+                from_hub(
+                    me, first, hub, members, rows, ((left_part, left_back),), part,
+                    (back_send.at[0],), (back_recv.at[0],),
+                )
+            if g > 0:
+                done = pl.ds((g - 1) * per, per)
+                drain(landed.at[done], swap_recv.at[g - 1])
+
+                @pl.loop((g - 1) * per, g * per)
+                def _(c):
+                    kept[c] = (
+                        kept[c].astype(jnp.float32) + landed[c].astype(jnp.float32)
+                    ).astype(jnp.bfloat16)
+
+                from_hub(
+                    me, first, hub, members, rows, ((kept, right_back),), done,
+                    (back_send.at[1],), (back_recv.at[1],),
                 )
 
     drain(left_back, back_recv.at[0])
     drain(right_back, back_recv.at[1])
-    others = pl.ds(0, n - 1)
-    drain(grad.at[others], send_sem)
-    drain(grad.at[others], back_send.at[0])
-    drain(grad.at[others], back_send.at[1])
+
+    @pl.when(is_hub)
+    def _():
+        drain(grad.at[pl.ds(0, hubs - 1)], send_sem)
+        drain(away, swap_send)
+        others = pl.ds(0, (members - 1) * rows)
+        drain(left_part.at[:, others, :], back_send.at[0])
+        drain(kept.at[:, others, :], back_send.at[1])
+
+    @pl.when(jnp.logical_not(is_hub))
+    def _():
+        drain(grad, send_sem)
 
 
 def totals_kernel(n, shares, totals, landed, mine, send_sem, recv_sem, back_send, back_recv):
@@ -212,20 +279,24 @@
     )
 
 
-def exchange_forward(left, right):
-    n, width, rows, residues = left.shape
+def exchange_forward(left, right, n):
+    hubs, width, rows, residues = left.shape
     chunks = min(CHUNKS, width)
-    slab = jax.ShapeDtypeStruct((width, n * rows, residues), jnp.bfloat16)
-    whole = jax.ShapeDtypeStruct((width, n * rows, n * rows), jnp.bfloat16)
     return pl.pallas_call(
         functools.partial(forward_kernel, n),
-        out_shape=[jax.ShapeDtypeStruct((n, width, rows, n * rows), jnp.bfloat16), slab, slab],
+        out_shape=[
+            jax.ShapeDtypeStruct((hubs, width, rows, n * rows), jnp.bfloat16),
+            jax.ShapeDtypeStruct((width, n // 2 * rows, residues), jnp.bfloat16),
+            jax.ShapeDtypeStruct((width, n * rows, residues), jnp.bfloat16),
+        ],
         in_specs=in_vmem(2),
         out_specs=in_vmem(3),
         scratch_shapes=[
-            pltpu.VMEM(whole.shape, jnp.bfloat16),
+            pltpu.VMEM((width, n // 2 * rows, n * rows), jnp.bfloat16),
             pltpu.SemaphoreType.DMA((2,)),
             pltpu.SemaphoreType.DMA((2, chunks)),
+            pltpu.SemaphoreType.DMA,
+            pltpu.SemaphoreType.DMA((chunks,)),
             pltpu.SemaphoreType.DMA,
             pltpu.SemaphoreType.DMA,
         ],
@@ -233,18 +304,22 @@
     )(left, right)
 
 
-def exchange_backward(grad, left_held, right_held):
-    n, width, rows, residues = grad.shape
+def exchange_backward(grad, left_held, right_held, n):
+    hubs, width, rows, _ = grad.shape
+    residues = left_held.shape[2]
     chunks = min(CHUNKS, width)
-    slab = (width, n * rows, residues)
-    back = jax.ShapeDtypeStruct((n, width, rows, residues), jnp.bfloat16)
+    slab = (width, n // 2 * rows, residues)
+    back = jax.ShapeDtypeStruct((hubs, width, rows, residues), jnp.bfloat16)
     return pl.pallas_call(
         functools.partial(backward_kernel, n),
         out_shape=[back, back],
         in_specs=in_vmem(3),
         out_specs=in_vmem(2),
-        scratch_shapes=[pltpu.VMEM(slab, jnp.bfloat16)] * 3
+        scratch_shapes=[pltpu.VMEM((width, n // 2 * rows, n * rows), jnp.bfloat16)]
+        + [pltpu.VMEM(slab, jnp.bfloat16)] * 4
         + [
+            pltpu.SemaphoreType.DMA,
+            pltpu.SemaphoreType.DMA((chunks,)),
             pltpu.SemaphoreType.DMA,
             pltpu.SemaphoreType.DMA((chunks,)),
             pltpu.SemaphoreType.DMA((2,)),
@@ -282,7 +357,8 @@
     local_rows = pair.shape[0]
     chans = pair.shape[2]
     ranks = lax.axis_size("rows")
-    slab_width = chans // ranks
+    hubs = ranks // 4
+    slab_width = chans // hubs
     normed_in, scale_in = layer_norm(pair.astype(jnp.float32), 2)
     normed_bf = normed_in.astype(jnp.bfloat16)
     edge_pre = jnp.einsum(
@@ -296,14 +372,14 @@
     left_edge = (
         (left_sig * edge_pre[0])
         .astype(jnp.bfloat16)
-        .reshape(ranks, slab_width, local_rows, residues)
+        .reshape(hubs, slab_width, local_rows, residues)
     )
     right_edge = (
         (right_sig * edge_pre[2])
         .astype(jnp.bfloat16)
-        .reshape(ranks, slab_width, local_rows, residues)
-    )
-    regrouped, left_held, right_held = exchange_forward(left_edge, right_edge)
+        .reshape(hubs, slab_width, local_rows, residues)
+    )
+    regrouped, left_held, right_held = exchange_forward(left_edge, right_edge, ranks)
     regrouped = regrouped.reshape(chans, local_rows, residues)
     normed_mid, scale_mid = layer_norm(regrouped.astype(jnp.float32), 0)
     mid_bf = normed_mid.astype(jnp.bfloat16)
@@ -325,8 +401,8 @@
         "ijd,cd->cij", gated_up, proj_weights[5], preferred_element_type=jnp.float32
     )
     prod_grad = norm_backward(normed_mid, scale_mid, mid_grad, 0).astype(jnp.bfloat16)
-    prod_grad = prod_grad.reshape(ranks, slab_width, local_rows, residues)
-    left_back, right_back = exchange_backward(prod_grad, left_held, right_held)
+    prod_grad = prod_grad.reshape(hubs, slab_width, local_rows, residues)
+    left_back, right_back = exchange_backward(prod_grad, left_held, right_held, ranks)
     left_full = left_back.reshape(chans, local_rows, residues).astype(jnp.float32)
     right_full = right_back.reshape(chans, local_rows, residues).astype(jnp.float32)
     edge_grad = jnp.stack(

time: 190 us -> 172 us (0.905)
  Pallas kernels: 162 us -> 144 us
    pallas_call x1, Pallas kernels: 73.2 us -> 65.2 us  [exchange_forward(): pl.pallas_call(functools.partial(forward_kernel, n), out_shape=[jax.Shape...]
    pallas_call x1, Pallas kernels: 69.9 us -> 63.1 us  [exchange_backward(): pl.pallas_call(functools.partial(backward_kernel, n), out_shape=[back, ba...]
    pallas_call x1, Pallas kernels: 18.5 us -> 15.5 us  [sum_over_rows(): pl.pallas_call(functools.partial(totals_kernel, n), out_shape=jax.ShapeDt...]
where the time goes in v2:
time: 172 us
  Pallas kernels  144 us (84%)
  other arithmetic  11.8 us (7%)
  matrix products  10.6 us (6%)
  local copies, waits for them, and re-layouts  5.27 us (3%)
    pallas_call x1, Pallas kernels, exchange_forward(): pl.pallas_call(functools.partial(forward_kernel, n), out_shape=[jax.Shape...  65.2 us
    pallas_call x1, Pallas kernels, exchange_backward(): pl.pallas_call(functools.partial(backward_kernel, n), out_shape=[back, ba...  63.1 us
    pallas_call x1, Pallas kernels, sum_over_rows(): pl.pallas_call(functools.partial(totals_kernel, n), out_shape=jax.ShapeDt...  15.5 us
    another operation x1, other arithmetic  5.35 us
    unnamed x6, local copies, waits for them, and re-layouts  3.51 us

profile of v2, /device:TPU:0, one launch (start us, length us, event | category | flops | bytes accessed | tf_op | source)
XLA Modules:
  0.0 172.3 jit_solution(16213092717610605242)
XLA Ops:
  0.6 0.0 copy-start.1
  0.6 1.5 copy.6
  2.2 0.2 convert_reduce_fusion
  2.4 0.3 fusion.9
  2.7 0.0 copy-done.1
  2.7 1.3 convolution_bitcast_fusion
  4.0 1.1 multiply_convert_fusion
  5.1 0.6 copy.11
  5.7 0.6 copy.10
  6.3 65.2 %shard_map.58 = (bf16[4,32,16,256]{3,2,1,0:T(8,128)(2,1)S(1)}, bf16[32,128,256]{2,1,0:T(8,128)(2,1)S(1)}, bf16[32,256,256]{2,1,0:T(8,128)(2,1)}) custom-call(bf16[4,32,16,256]{3,2,1,0:T(8,128)(2,1)S(1)} %bitcast.98, bf16[4,32,16,256]{3,2,1,0:T(8,128)(2,1)S(1)} %bitcast.97), custom_call_target="tpu_custom_call" | custom-call | tf_op jit(solution)/shard_map/pallas_call | solution.py:285
  71.5 0.2 convert_reduce_fusion.1
  71.7 0.3 multiply_reduce_fusion
  72.1 0.3 multiply_convert_fusion.7
  72.3 0.3 bitcast_convert_fusion.2
  72.7 0.0 copy-start
  72.7 0.6 fusion.35
  73.2 0.7 copy-done
  73.9 2.2 %fusion.13 = (bf16[16,256,128]{2,1,0:T(8,128)(2,1)S(1)}, bf16[16,256,128]{2,1,0:T(8,128)(2,1)}, f32[16,256,128]{2,1,0:T(8,128)S(1)}) fusion(f32[16,256,128]{2,1,0:T(8,128)S(1)} %fusion.35, bf16[16,256,128]{2,1,0:T(8,128)(2,1)S(1)} %copy-done, bf16[6,128,128]{2,1,0:T(8,128)(2,1)S(1)} %copy-done.1, bf16[16,256,128]{1,2,0:T(8,128)(2,1)S(1)} %copy.6, ...), kind=kOutput, calls=%fused_computation.19 | convolution fusion | flops 142082048 | bytes 8454144 | tf_op jit(solution)/shard_map/ikd,dc->ikc/dot_general | solution.py:367
  76.1 0.4 fusion.31
  76.5 1.5 fusion.30
  78.1 1.7 bitcast_reduce_fusion
  79.8 1.7 fusion.22
  81.5 0.6 copy.14
  82.0 63.1 %shard_map.59 = (bf16[4,32,16,256]{3,2,1,0:T(8,128)(2,1)S(1)}, bf16[4,32,16,256]{3,2,1,0:T(8,128)(2,1)S(1)}) custom-call(bf16[4,32,16,256]{3,2,1,0:T(8,128)(2,1)S(1)} %bitcast.96, bf16[32,128,256]{2,1,0:T(8,128)(2,1)S(1)} %get-tuple-element.9.left_held, bf16[32,256,256]{2,1,0:T(8,128)(2,1)} %get-tuple-element.10.right_held), custom_call_target="tpu_custom_call" | custom-call | tf_op jit(solution)/shard_map/pallas_call | solution.py:313
  145.1 0.3 bitcast_convert_fusion
  145.4 0.3 bitcast_convert_fusion.1
  145.7 5.4 %multiply_convert_fusion.5 = (bf16[1,128,16,256]{3,1,0,2:T(8,128)(2,1)S(1)}, bf16[1,128,16,256]{3,1,0,2:T(8,128)(2,1)S(1)}, bf16[1,128,16,256]{3,1,0,2:T(8,128)(2,1)S(1)}, bf16[1,128,16,256]{3,1,0,2:T(8,128)(2,1)S(1)}) fusion(f32[1,128,16,256]{3,2,1,0:T(8,128)S(1)} %bitcast_convert_fusion.1, f32[4,128,16,256]{3,1,0,2:T(8,128)S(1)} %convolution_bitcast_fusion, ...), kind=kLoop, calls=%fused_computation.43 | loop fusion | flops 10485760 | bytes 16777216 | tf_op jit(solution)/shard_map/convert.9
  151.1 1.5 fusion.27
  152.6 0.7 fusion.39
  153.3 0.7 fusion.61
  154.0 15.5 %shard_map.60 = bf16[16,48,128]{2,1,0:T(8,128)(2,1)S(1)} custom-call(bf16[16,48,128]{2,1,0:T(8,128)(2,1)S(1)} %bitcast.101), custom_call_target="tpu_custom_call" | custom-call | tf_op jit(solution)/shard_map/pallas_call | solution.py:337
  169.6 0.6 fusion.8
  170.2 1.3 copy.21
  171.5 0.8 convert_multiply_fusion.2
  (8 shorter events, 0.1 us)
Async XLA Ops:
  0.6 2.1 %copy-start.1 = (bf16[6,128,128]{2,1,0:T(8,128)(2,1)S(1)}, bf16[6,128,128]{2,1,0:T(8,128)(2,1)}, u32[]{:S(2)}) copy-start(bf16[6,128,128]{2,1,0:T(8,128)(2,1)} %param.4) | copy-start | bytes 589828
  72.7 1.2 copy-start

commit v3 on v2

--- a/solution.py
+++ b/solution.py
@@ -8,7 +8,7 @@
 from jax.sharding import PartitionSpec as P
 
 VMEM_LIMIT = 48 * 1024 * 1024
-CHUNKS = 8
+CHUNKS = 16
 
 
 def layer_norm(values, along_dim):

time: 172 us -> 167 us (0.971)
  Pallas kernels: 144 us -> 138 us
    pallas_call x1, Pallas kernels: 15.5 us -> 12.9 us  [sum_over_rows(): pl.pallas_call(functools.partial(totals_kernel, n), out_shape=jax.ShapeDt...]
where the time goes in v3:
time: 167 us
  Pallas kernels  138 us (83%)
  other arithmetic  11.8 us (7%)
  matrix products  10.6 us (6%)
  local copies, waits for them, and re-layouts  5.27 us (3%)
    pallas_call x1, Pallas kernels, exchange_forward(): pl.pallas_call(functools.partial(forward_kernel, n), out_shape=[jax.Shape...  63.6 us
    pallas_call x1, Pallas kernels, exchange_backward(): pl.pallas_call(functools.partial(backward_kernel, n), out_shape=[back, ba...  61.7 us
    pallas_call x1, Pallas kernels, sum_over_rows(): pl.pallas_call(functools.partial(totals_kernel, n), out_shape=jax.ShapeDt...  12.9 us
    another operation x1, other arithmetic  5.35 us
    unnamed x6, local copies, waits for them, and re-layouts  3.51 us

profile of v3, /device:TPU:0, one launch (start us, length us, event | category | flops | bytes accessed | tf_op | source)
XLA Modules:
  0.0 166.7 jit_solution(15746790944027432765)
XLA Ops:
  0.6 0.0 copy-start.1
  0.6 1.5 copy.6
  2.2 0.2 convert_reduce_fusion
  2.4 0.3 fusion.9
  2.7 0.0 copy-done.1
  2.7 1.3 convolution_bitcast_fusion
  4.0 1.1 multiply_convert_fusion
  5.1 0.6 copy.11
  5.7 0.6 copy.10
  6.3 63.6 %shard_map.58 = (bf16[4,32,16,256]{3,2,1,0:T(8,128)(2,1)S(1)}, bf16[32,128,256]{2,1,0:T(8,128)(2,1)S(1)}, bf16[32,256,256]{2,1,0:T(8,128)(2,1)}) custom-call(bf16[4,32,16,256]{3,2,1,0:T(8,128)(2,1)S(1)} %bitcast.98, bf16[4,32,16,256]{3,2,1,0:T(8,128)(2,1)S(1)} %bitcast.97), custom_call_target="tpu_custom_call" | custom-call | tf_op jit(solution)/shard_map/pallas_call | solution.py:285
  69.9 0.2 convert_reduce_fusion.1
  70.1 0.3 multiply_reduce_fusion
  70.4 0.3 multiply_convert_fusion.7
  70.7 0.3 bitcast_convert_fusion.2
  71.0 0.0 copy-start
  71.1 0.6 fusion.35
  71.6 0.7 copy-done
  72.3 2.2 %fusion.13 = (bf16[16,256,128]{2,1,0:T(8,128)(2,1)S(1)}, bf16[16,256,128]{2,1,0:T(8,128)(2,1)}, f32[16,256,128]{2,1,0:T(8,128)S(1)}) fusion(f32[16,256,128]{2,1,0:T(8,128)S(1)} %fusion.35, bf16[16,256,128]{2,1,0:T(8,128)(2,1)S(1)} %copy-done, bf16[6,128,128]{2,1,0:T(8,128)(2,1)S(1)} %copy-done.1, bf16[16,256,128]{1,2,0:T(8,128)(2,1)S(1)} %copy.6, ...), kind=kOutput, calls=%fused_computation.19 | convolution fusion | flops 142082048 | bytes 8454144 | tf_op jit(solution)/shard_map/ikd,dc->ikc/dot_general | solution.py:367
  74.5 0.4 fusion.31
  74.9 1.5 fusion.30
  76.4 1.7 %bitcast_reduce_fusion = (f32[16,256]{1,0:T(8,128)S(1)}, f32[16,256]{1,0:T(8,128)S(1)}, f32[16,256,128]{1,2,0:T(8,128)S(1)}) fusion(f32[16,256]{1,0:T(8,128)S(1)} %add_rsqrt_fusion, f32[16,256]{1,0:T(8,128)S(1)} %broadcast_multiply_fusion.4, f32[128,16,256]{2,1,0:T(8,128)S(1)} %bitcast_convert_fusion.2, bf16[6,128,128]{2,1,0:T(8,128)(2,1)S(1)} %copy-done.1, ...), kind=kOutput, calls=%fused_computation.31 | convolution fusion | flops 138403840 | bytes 7438336 | tf_op jit(solution)/shard_map/ijd,cd->cij/dot_general | solution.py:400
  78.1 1.7 %fusion.22 = bf16[128,16,256]{2,0,1:T(8,128)(2,1)S(1)} fusion(f32[16,256,128]{1,2,0:T(8,128)S(1)} %get-tuple-element.31, f32[128,16,256]{2,1,0:T(8,128)S(1)} %bitcast_convert_fusion.2, f32[16,256]{1,0:T(8,128)S(1)} %get-tuple-element.33, f32[16,256]{1,0:T(8,128)S(1)} %add_rsqrt_fusion, f32[16,256]{1,0:T(8,128)S(1)} %broadcast_multiply_fusion.4, ...), kind=kLoop, calls=%fused_computation.34 | loop fusion | flops 3670016 | bytes 5308416 | tf_op jit(solution)/shard_map/convert_element_type | solution.py:403
  79.8 0.6 copy.14
  80.4 61.7 %shard_map.59 = (bf16[4,32,16,256]{3,2,1,0:T(8,128)(2,1)S(1)}, bf16[4,32,16,256]{3,2,1,0:T(8,128)(2,1)S(1)}) custom-call(bf16[4,32,16,256]{3,2,1,0:T(8,128)(2,1)S(1)} %bitcast.96, bf16[32,128,256]{2,1,0:T(8,128)(2,1)S(1)} %get-tuple-element.9.left_held, bf16[32,256,256]{2,1,0:T(8,128)(2,1)} %get-tuple-element.10.right_held), custom_call_target="tpu_custom_call" | custom-call | tf_op jit(solution)/shard_map/pallas_call | solution.py:313
  142.1 0.3 bitcast_convert_fusion
  142.4 0.3 bitcast_convert_fusion.1
  142.7 5.4 %multiply_convert_fusion.5 = (bf16[1,128,16,256]{3,1,0,2:T(8,128)(2,1)S(1)}, bf16[1,128,16,256]{3,1,0,2:T(8,128)(2,1)S(1)}, bf16[1,128,16,256]{3,1,0,2:T(8,128)(2,1)S(1)}, bf16[1,128,16,256]{3,1,0,2:T(8,128)(2,1)S(1)}) fusion(f32[1,128,16,256]{3,2,1,0:T(8,128)S(1)} %bitcast_convert_fusion.1, f32[4,128,16,256]{3,1,0,2:T(8,128)S(1)} %convolution_bitcast_fusion, ...), kind=kLoop, calls=%fused_computation.43 | loop fusion | flops 10485760 | bytes 16777216 | tf_op jit(solution)/shard_map/convert.9
  148.0 1.5 fusion.27
  149.6 0.7 fusion.39
  150.3 0.7 fusion.61
  151.0 12.9 %shard_map.60 = bf16[16,48,128]{2,1,0:T(8,128)(2,1)S(1)} custom-call(bf16[16,48,128]{2,1,0:T(8,128)(2,1)S(1)} %bitcast.101), custom_call_target="tpu_custom_call" | custom-call | tf_op jit(solution)/shard_map/pallas_call | solution.py:337
  164.0 0.6 fusion.8
  164.6 1.3 copy.21
  165.9 0.8 convert_multiply_fusion.2
  (8 shorter events, 0.1 us)
Async XLA Ops:
  0.6 2.1 %copy-start.1 = (bf16[6,128,128]{2,1,0:T(8,128)(2,1)S(1)}, bf16[6,128,128]{2,1,0:T(8,128)(2,1)}, u32[]{:S(2)}) copy-start(bf16[6,128,128]{2,1,0:T(8,128)(2,1)} %param.4) | copy-start | bytes 589828
  71.0 1.2 copy-start

commit v4 on v3

--- a/solution.py
+++ b/solution.py
@@ -8,7 +8,19 @@
 from jax.sharding import PartitionSpec as P
 
 VMEM_LIMIT = 48 * 1024 * 1024
-CHUNKS = 16
+EDGE = (2, 2, 2, 2)
+FORWARD_CHUNK = 2
+BACKWARD_CHUNK = 4
+
+
+def cut(width, inner):
+    room = width - 2 * sum(EDGE)
+    if room < 0 or room % inner:
+        sizes = (1,) * width
+    else:
+        sizes = EDGE + (inner,) * (room // inner) + EDGE[::-1]
+    bounds = [sum(sizes[:g]) for g in range(len(sizes) + 1)]
+    return list(zip(bounds[:-1], bounds[1:]))
 
 
 def layer_norm(values, along_dim):
@@ -63,6 +75,32 @@
     is_hub = jnp.logical_and(me >= hub, me < hub + n // 4)
     partner = me + n // 4 * (1 - 2 * half)
     return me, half, first, hub, is_hub, partner
+
+
+def meet_partners(n, me, first, hub, is_hub, partner):
+    barrier = pltpu.get_barrier_semaphore()
+
+    def greet(rank):
+        pl.semaphore_signal(
+            barrier, inc=1, device_id={"rows": rank}, device_id_type=pl.DeviceIdType.MESH
+        )
+
+    @pl.when(is_hub)
+    def _():
+        @pl.loop(1, n // 2)
+        def _(s):
+            greet(first + lax.rem(me - first + s, n // 2))
+
+        greet(partner)
+        pl.semaphore_wait(barrier, n // 2)
+
+    @pl.when(jnp.logical_not(is_hub))
+    def _():
+        @pl.loop(0, n // 4)
+        def _(s):
+            greet(hub + s)
+
+        pl.semaphore_wait(barrier, n // 4)
 
 
 def to_hubs(me, hub, hubs, is_hub, pairs, part, send_sems, recv_sems):
@@ -107,13 +145,14 @@
     me, half, first, hub, is_hub, partner = place(n)
     hubs, width, rows, _ = left.shape
     members = n // 2
-    chunks = swap_recv.shape[0]
-    per = width // chunks
-    meet(n, me)
+    bounds = cut(width, FORWARD_CHUNK)
+    chunks = len(bounds)
+    parts = [pl.ds(a, b - a) for a, b in bounds]
+    meet_partners(n, me, first, hub, is_hub, partner)
     own_rows = pl.ds(first * rows, members * rows)
     far_rows = pl.ds((members - first) * rows, members * rows)
     for g in range(chunks):
-        part = pl.ds(g * per, per)
+        part = parts[g]
         pairs = (
             (right, right_held.at[part, pl.ds(me * rows, rows), :]),
             (left, left_held.at[part, pl.ds((me - first) * rows, rows), :]),
@@ -127,16 +166,16 @@
     def _():
         for g in range(chunks + 1):
             if g < chunks:
-                part = pl.ds(g * per, per)
+                part = parts[g]
                 block = right_held.at[part, own_rows, :]
                 drain(block, recv_sem.at[1, g])
                 send(block, block, swap_send, swap_recv.at[g], partner)
             if g > 0:
-                done = pl.ds((g - 1) * per, per)
+                done = parts[g - 1]
                 drain(left_held.at[done], recv_sem.at[0, g - 1])
                 drain(right_held.at[done, far_rows, :], swap_recv.at[g - 1])
 
-                @pl.loop((g - 1) * per, g * per)
+                @pl.loop(*bounds[g - 1])
                 def _(c):
                     products[c] = lax.dot_general(
                         left_held[c], right_held[c], (((1,), (1,)), ((), ())),
@@ -172,14 +211,15 @@
     me, half, first, hub, is_hub, partner = place(n)
     hubs, width, rows, _ = grad.shape
     members = n // 2
-    chunks = swap_recv.shape[0]
-    per = width // chunks
-    meet(n, me)
+    bounds = cut(width, BACKWARD_CHUNK)
+    chunks = len(bounds)
+    parts = [pl.ds(a, b - a) for a, b in bounds]
+    meet_partners(n, me, first, hub, is_hub, partner)
     span = members * rows
     own_cols = pl.ds(pl.multiple_of(first * rows, span), span)
     far_cols = pl.ds(pl.multiple_of((members - first) * rows, span), span)
     for g in range(chunks):
-        part = pl.ds(g * per, per)
+        part = parts[g]
         pairs = ((grad, held.at[part, pl.ds((me - first) * rows, rows), :]),)
         to_hubs(me, hub, hubs, is_hub, pairs, part, (send_sem,), (recv_sem.at[g],))
 
@@ -192,16 +232,16 @@
     def _():
         for g in range(chunks + 1):
             if g < chunks:
-                part = pl.ds(g * per, per)
+                part = parts[g]
                 drain(held.at[part], recv_sem.at[g])
 
-                @pl.loop(g * per, (g + 1) * per)
+                @pl.loop(*bounds[g])
                 def _(c):
                     away[c] = outer(held[c, :, far_cols], left_held[c])
 
                 send(away.at[part], landed.at[part], swap_send, swap_recv.at[g], partner)
 
-                @pl.loop(g * per, (g + 1) * per)
+                @pl.loop(*bounds[g])
                 def _(c):
                     left_part[c] = lax.dot_general(
                         held[c], right_held[c], (((1,), (0,)), ((), ())),
@@ -214,10 +254,10 @@
                     (back_send.at[0],), (back_recv.at[0],),
                 )
             if g > 0:
-                done = pl.ds((g - 1) * per, per)
+                done = parts[g - 1]
                 drain(landed.at[done], swap_recv.at[g - 1])
 
-                @pl.loop((g - 1) * per, g * per)
+                @pl.loop(*bounds[g - 1])
                 def _(c):
                     kept[c] = (
                         kept[c].astype(jnp.float32) + landed[c].astype(jnp.float32)
@@ -281,7 +321,7 @@
 
 def exchange_forward(left, right, n):
     hubs, width, rows, residues = left.shape
-    chunks = min(CHUNKS, width)
+    chunks = len(cut(width, FORWARD_CHUNK))
     return pl.pallas_call(
         functools.partial(forward_kernel, n),
         out_shape=[
@@ -307,7 +347,7 @@
 def exchange_backward(grad, left_held, right_held, n):
     hubs, width, rows, _ = grad.shape
     residues = left_held.shape[2]
-    chunks = min(CHUNKS, width)
+    chunks = len(cut(width, BACKWARD_CHUNK))
     slab = (width, n // 2 * rows, residues)
     back = jax.ShapeDtypeStruct((hubs, width, rows, residues), jnp.bfloat16)
     return pl.pallas_call(

time: 167 us -> 167 us (level)
  no operation moved by 1% of the time
where the time goes in v4:
time: 167 us; the launch traced here: 166 us
  Pallas kernels  138 us (83%)
  other arithmetic  11.8 us (7%)
  matrix products  10.6 us (6%)
  local copies, waits for them, and re-layouts  5.27 us (3%)
    pallas_call x1, Pallas kernels, exchange_forward(): pl.pallas_call(functools.partial(forward_kernel, n), out_shape=[jax.Shape...  62.6 us
    pallas_call x1, Pallas kernels, exchange_backward(): pl.pallas_call(functools.partial(backward_kernel, n), out_shape=[back, ba...  61.6 us
    pallas_call x1, Pallas kernels, sum_over_rows(): pl.pallas_call(functools.partial(totals_kernel, n), out_shape=jax.ShapeDt...  13.7 us
    another operation x1, other arithmetic  5.35 us
    unnamed x6, local copies, waits for them, and re-layouts  3.51 us

profile of v4, /device:TPU:0, one launch (start us, length us, event | category | flops | bytes accessed | tf_op | source)
XLA Modules:
  0.0 166.4 jit_solution(4841954680787481838)
XLA Ops:
  0.6 0.0 copy-start.1
  0.6 1.5 copy.6
  2.2 0.2 convert_reduce_fusion
  2.4 0.3 fusion.9
  2.7 0.0 copy-done.1
  2.7 1.3 convolution_bitcast_fusion
  4.0 1.1 multiply_convert_fusion
  5.1 0.6 copy.11
  5.7 0.6 copy.10
  6.3 62.6 %shard_map.58 = (bf16[4,32,16,256]{3,2,1,0:T(8,128)(2,1)S(1)}, bf16[32,128,256]{2,1,0:T(8,128)(2,1)S(1)}, bf16[32,256,256]{2,1,0:T(8,128)(2,1)}) custom-call(bf16[4,32,16,256]{3,2,1,0:T(8,128)(2,1)S(1)} %bitcast.98, bf16[4,32,16,256]{3,2,1,0:T(8,128)(2,1)S(1)} %bitcast.97), custom_call_target="tpu_custom_call" | custom-call | tf_op jit(solution)/shard_map/pallas_call | solution.py:325
  68.9 0.2 convert_reduce_fusion.1
  69.1 0.3 multiply_reduce_fusion
  69.5 0.3 multiply_convert_fusion.7
  69.7 0.3 bitcast_convert_fusion.2
  70.1 0.0 copy-start
  70.1 0.6 fusion.35
  70.6 0.7 copy-done
  71.3 2.2 %fusion.13 = (bf16[16,256,128]{2,1,0:T(8,128)(2,1)S(1)}, bf16[16,256,128]{2,1,0:T(8,128)(2,1)}, f32[16,256,128]{2,1,0:T(8,128)S(1)}) fusion(f32[16,256,128]{2,1,0:T(8,128)S(1)} %fusion.35, bf16[16,256,128]{2,1,0:T(8,128)(2,1)S(1)} %copy-done, bf16[6,128,128]{2,1,0:T(8,128)(2,1)S(1)} %copy-done.1, bf16[16,256,128]{1,2,0:T(8,128)(2,1)S(1)} %copy.6, ...), kind=kOutput, calls=%fused_computation.19 | convolution fusion | flops 142082048 | bytes 8454144 | tf_op jit(solution)/shard_map/ikd,dc->ikc/dot_general | solution.py:407
  73.5 0.4 fusion.31
  73.9 1.5 fusion.30
  75.5 1.7 %bitcast_reduce_fusion = (f32[16,256]{1,0:T(8,128)S(1)}, f32[16,256]{1,0:T(8,128)S(1)}, f32[16,256,128]{1,2,0:T(8,128)S(1)}) fusion(f32[16,256]{1,0:T(8,128)S(1)} %add_rsqrt_fusion, f32[16,256]{1,0:T(8,128)S(1)} %broadcast_multiply_fusion.4, f32[128,16,256]{2,1,0:T(8,128)S(1)} %bitcast_convert_fusion.2, bf16[6,128,128]{2,1,0:T(8,128)(2,1)S(1)} %copy-done.1, ...), kind=kOutput, calls=%fused_computation.31 | convolution fusion | flops 138403840 | bytes 7438336 | tf_op jit(solution)/shard_map/ijd,cd->cij/dot_general | solution.py:440
  77.2 1.7 %fusion.22 = bf16[128,16,256]{2,0,1:T(8,128)(2,1)S(1)} fusion(f32[16,256,128]{1,2,0:T(8,128)S(1)} %get-tuple-element.31, f32[128,16,256]{2,1,0:T(8,128)S(1)} %bitcast_convert_fusion.2, f32[16,256]{1,0:T(8,128)S(1)} %get-tuple-element.33, f32[16,256]{1,0:T(8,128)S(1)} %add_rsqrt_fusion, f32[16,256]{1,0:T(8,128)S(1)} %broadcast_multiply_fusion.4, ...), kind=kLoop, calls=%fused_computation.34 | loop fusion | flops 3670016 | bytes 5308416 | tf_op jit(solution)/shard_map/convert_element_type | solution.py:443
  78.9 0.6 copy.14
  79.4 61.6 %shard_map.59 = (bf16[4,32,16,256]{3,2,1,0:T(8,128)(2,1)S(1)}, bf16[4,32,16,256]{3,2,1,0:T(8,128)(2,1)S(1)}) custom-call(bf16[4,32,16,256]{3,2,1,0:T(8,128)(2,1)S(1)} %bitcast.96, bf16[32,128,256]{2,1,0:T(8,128)(2,1)S(1)} %get-tuple-element.9.left_held, bf16[32,256,256]{2,1,0:T(8,128)(2,1)} %get-tuple-element.10.right_held), custom_call_target="tpu_custom_call" | custom-call | tf_op jit(solution)/shard_map/pallas_call | solution.py:353
  141.0 0.3 bitcast_convert_fusion
  141.3 0.3 bitcast_convert_fusion.1
  141.6 5.4 %multiply_convert_fusion.5 = (bf16[1,128,16,256]{3,1,0,2:T(8,128)(2,1)S(1)}, bf16[1,128,16,256]{3,1,0,2:T(8,128)(2,1)S(1)}, bf16[1,128,16,256]{3,1,0,2:T(8,128)(2,1)S(1)}, bf16[1,128,16,256]{3,1,0,2:T(8,128)(2,1)S(1)}) fusion(f32[1,128,16,256]{3,2,1,0:T(8,128)S(1)} %bitcast_convert_fusion.1, f32[4,128,16,256]{3,1,0,2:T(8,128)S(1)} %convolution_bitcast_fusion, ...), kind=kLoop, calls=%fused_computation.43 | loop fusion | flops 10485760 | bytes 16777216 | tf_op jit(solution)/shard_map/convert.9
  147.0 1.5 fusion.27
  148.5 0.7 fusion.39
  149.3 0.7 fusion.61
  150.0 13.7 %shard_map.60 = bf16[16,48,128]{2,1,0:T(8,128)(2,1)S(1)} custom-call(bf16[16,48,128]{2,1,0:T(8,128)(2,1)S(1)} %bitcast.101), custom_call_target="tpu_custom_call" | custom-call | tf_op jit(solution)/shard_map/pallas_call | solution.py:377
  163.7 0.6 fusion.8
  164.3 1.3 copy.21
  165.6 0.8 convert_multiply_fusion.2
  (8 shorter events, 0.1 us)
Async XLA Ops:
  0.6 2.1 %copy-start.1 = (bf16[6,128,128]{2,1,0:T(8,128)(2,1)S(1)}, bf16[6,128,128]{2,1,0:T(8,128)(2,1)}, u32[]{:S(2)}) copy-start(bf16[6,128,128]{2,1,0:T(8,128)(2,1)} %param.4) | copy-start | bytes 589828
  70.1 1.2 copy-start
